TPU v7x, 256 devices: a whole 4x4x8 slice. The times are simulated.
256 devices in a mesh: vocab: 64 (over z, y, core), tok: 4 (over x).
Axes of the slice: x: 4, y: 4, z: 8, core: 2. Of those that a mesh axis runs over, the one named last changes fastest.
Arguments:
- hidden: bfloat16 [1024, 3584], P('vocab', 'tok'), may hold values from -18 to 18
- head: bfloat16 [3584, 131072], P('tok', 'vocab'), may hold values from -0.15033445 to 0.15033445
- teacher: bfloat16 [1024, 131072], P(('tok', 'vocab')), may hold values from -18 to 320
- token_weight: float32 [1024], P('tok'), may hold values from 64 to 512
Outputs:
- grad_hidden: bfloat16 [1024, 3584], P('vocab', 'tok')
- grad_head: bfloat16 [3584, 131072], P('tok', 'vocab')
All inputs are finite; a program needn't handle non-finite values.
Results may differ from a plain program's by a relative error of at most 0.0065.
Values may be sent and summed in bfloat16 or wider, within the bound.
A program may use at most 64 MiB of HBM per device.

v0:
```python
import jax
import jax.numpy as jnp
from jax import lax
from jax.sharding import PartitionSpec as P


def body(hidden, head, teacher, token_weight):
    rows_all = lax.all_gather(hidden, "vocab", axis=0, tiled=True)
    logits = lax.psum_scatter(
        jnp.dot(rows_all, head, preferred_element_type=jnp.float32),
        "tok",
        scatter_dimension=0,
        tiled=True,
    )
    target_logits = lax.all_to_all(
        teacher, "vocab", split_axis=1, concat_axis=0, tiled=True
    ).astype(jnp.float32)
    student_peak, target_peak = lax.pmax(
        (jnp.max(logits, axis=1), jnp.max(target_logits, axis=1)), "vocab"
    )
    student_exp = jnp.exp(logits - student_peak[:, None])
    target_exp = jnp.exp(target_logits - target_peak[:, None])
    student_total, target_total = lax.psum(
        (jnp.sum(student_exp, axis=1), jnp.sum(target_exp, axis=1)), "vocab"
    )
    student = student_exp / student_total[:, None]
    target = target_exp / target_total[:, None]
    grad_logits = (token_weight[:, None] * (student - target)).astype(jnp.bfloat16)
    grad_all = lax.all_gather(grad_logits, "tok", axis=0, tiled=True)
    grad_head = lax.dot_general(
        rows_all, grad_all, (((0,), (0,)), ((), ())), preferred_element_type=jnp.float32
    ).astype(jnp.bfloat16)
    partial_input = lax.dot_general(
        grad_all, head, (((1,), (1,)), ((), ())), preferred_element_type=jnp.float32
    )
    summed = lax.psum(partial_input, "vocab")
    share = summed.shape[0] // lax.axis_size("vocab")
    grad_input = lax.dynamic_slice_in_dim(summed, lax.axis_index("vocab") * share, share, 0)
    return (grad_input.astype(jnp.bfloat16), grad_head)


def solution(mesh):
    return jax.shard_map(
        body,
        mesh=mesh,
        in_specs=(P("vocab", "tok"), P("tok", "vocab"), P(("tok", "vocab"), None), P("tok")),
        out_specs=(P("vocab", "tok"), P("tok", "vocab")),
        check_vma=False,
    )
```

profile of v0, /device:TPU:2, one launch (start us, length us, event | category | flops | bytes accessed | tf_op | source)
XLA Modules:
  0.0 808.6 jit_solution(6296472803187103812)
XLA Ops:
  7.2 0.0 all-gather.3.cloned.1.call-start
  7.2 0.7 all-gather.3.cloned.1.call-update
  7.9 0.0 reduce-scatter.2.cloned.1.call-start
  7.9 82.8 %all-gather.3.cloned.1.call-done = bf16[1024,896]{1,0:T(8,128)(2,1)} async-done(((bf16[16,896]{1,0:T(8,128)(2,1)}), bf16[1024,896]{1,0:T(8,128)(2,1)}) %all-gather.3.cloned.1.call-update) | async-done | bytes 1835024 | tf_op jit(solution)/shard_map/all_gather | solution.py:8
  90.7 10.3 %fusion.1 = f32[1024,2048]{1,0:T(8,128)} fusion(bf16[1024,896]{1,0:T(8,128)(2,1)} %all-gather.3.cloned.1.call-done, bf16[896,2048]{1,0:T(8,128)(2,1)} %param.5), kind=kOutput, calls=%fused_computation.8 | convolution fusion | flops 3758096384 | bytes 13893632 | tf_op jit(solution)/shard_map/dot_general | solution.py:10
  101.0 0.0 copy-start.1
  101.0 0.0 reduce-scatter.2.cloned.1.call-update
  101.1 0.0 all-gather.5.cloned.1.call-start
  101.1 1.1 copy-done.1
  102.3 35.6 %all_to_all.16 = bf16[4,64,2048]{2,0,1:T(4,128)(2,1)S(1)} all-to-all(bf16[4,64,2048]{2,0,1:T(4,128)(2,1)S(1)} %bitcast.14), channel_id=1, replica_groups=mesh['vocab'=64,'tok'=4] {'vocab'}, dimensions={1} | all-to-all | bytes 2097152 | tf_op jit(solution)/shard_map/all_to_all | solution.py:15
  137.8 0.5 bitcast_reduce_fusion
  138.3 0.1 reshape.23
  138.4 0.2 bitcast_convert_fusion
  138.6 1.7 reshape.22
  140.4 40.3 %reduce-scatter.2.cloned.1.call-done = f32[256,2048]{1,0:T(8,128)} async-done(((f32[1024,2048]{1,0:T(8,128)}), f32[256,2048]{1,0:T(8,128)}) %reduce-scatter.2.cloned.1.call-update) | async-done | bytes 2097168 | tf_op jit(solution)/shard_map/reduce_scatter | solution.py:9
  180.7 1.9 reduce_max.25
  182.7 129.0 %all-reduce.1 = (f32[256]{0:T(256)S(1)}, f32[256]{0:T(256)S(1)}) all-reduce(f32[256]{0:T(256)S(1)} %reshape.23, f32[256]{0:T(256)S(1)} %reduce_max.25), channel_id=1, replica_groups=mesh['vocab'=64,'tok'=4] {'vocab'}, use_global_device_ids=true, to_apply=%region_6.0 | all-reduce | flops 512 | bytes 4096 | tf_op jit(solution)/shard_map/pmax | solution.py:18
  311.7 0.1 sub.30
  311.8 1.0 exponential_reduce_fusion
  312.8 0.1 reduce_sum.22
  312.9 0.0 copy-done
  312.9 0.4 fusion
  313.3 124.1 %all-reduce = (f32[256]{0:T(256)S(1)}, f32[256]{0:T(256)S(1)}) all-reduce(f32[256]{0:T(256)S(1)} %reduce_sum.22, f32[256]{0:T(256)S(1)} %fusion), channel_id=1, replica_groups=mesh['vocab'=64,'tok'=4] {'vocab'}, use_global_device_ids=true, to_apply=%region_8.0 | all-reduce | flops 512 | bytes 4096 | tf_op jit(solution)/shard_map/psum | solution.py:23
  437.4 0.0 copy-done.2
  437.4 3.4 multiply_convert_fusion
  440.8 0.0 all-gather.5.cloned.1.call-update
  440.8 46.0 %all-gather.5.cloned.1.call-done = bf16[1024,2048]{1,0:T(8,128)(2,1)} async-done(((bf16[256,2048]{1,0:T(8,128)(2,1)}), bf16[1024,2048]{1,0:T(8,128)(2,1)}) %all-gather.5.cloned.1.call-update) | async-done | bytes 4194320 | tf_op jit(solution)/shard_map/all_gather | solution.py:29
  486.9 9.7 %fusion.2 = f32[1024,896]{1,0:T(8,128)} fusion(bf16[1024,2048]{1,0:T(8,128)(2,1)} %all-gather.5.cloned.1.call-done, bf16[896,2048]{1,0:T(8,128)(2,1)} %param.5), kind=kOutput, calls=%fused_computation.9 | convolution fusion | flops 3758096384 | bytes 11534336 | tf_op jit(solution)/shard_map/dot_general | solution.py:33
  496.5 289.7 %all-reduce.3 = bf16[1024,896]{1,0:T(8,128)(2,1)S(1)} all-reduce(f32[1024,896]{1,0:T(8,128)} %fusion.2), channel_id=1, replica_groups=mesh['vocab'=64,'tok'=4] {'vocab'}, use_global_device_ids=true, to_apply=%region_9.0 | all-reduce | flops 917504 | bytes 5505024 | tf_op jit(solution)/shard_map/psum | solution.py:36
  786.2 9.2 %convert_bitcast_fusion = bf16[896,2048]{0,1:T(8,128)(2,1)} fusion(bf16[1024,2048]{1,0:T(8,128)(2,1)} %all-gather.5.cloned.1.call-done, bf16[1024,896]{1,0:T(8,128)(2,1)} %all-gather.3.cloned.1.call-done), kind=kOutput, calls=%fused_computation | convolution fusion | flops 3759931392 | bytes 9699328 | tf_op jit(solution)/shard_map/dot_general | solution.py:30
  795.4 6.0 copy.9
  801.5 0.6 dynamic-slice_convert_fusion
  (2 shorter events, 0.0 us)
Async XLA Ops:
  7.2 83.6 %all-gather.3.cloned.1.call-start = ((), (), s32[]{:S(2)}) async-start(), calls=%async_computation.2 | async-start | bytes 1863680 | tf_op jit(solution)/shard_map/all_gather | solution.py:8
  7.9 172.8 %reduce-scatter.2.cloned.1.call-start = ((), (), s32[]{:S(2)}) async-start(), calls=%async_computation.3 | async-start | bytes 10485760 | tf_op jit(solution)/shard_map/reduce_scatter | solution.py:9
  101.0 1.2 copy-start.1
  101.1 385.8 %all-gather.5.cloned.1.call-start = ((), (), s32[]{:S(2)}) async-start(), calls=%async_computation.4 | async-start | bytes 5242880 | tf_op jit(solution)/shard_map/all_gather | solution.py:29
  180.7 132.2 %copy-start = (f32[256,2048]{1,0:T(8,128)S(1)}, f32[256,2048]{1,0:T(8,128)}, u32[]{:S(2)}) copy-start(f32[256,2048]{1,0:T(8,128)} %reduce-scatter.2.cloned.1.call-done) | copy-start | bytes 6291460
  182.6 254.7 %copy-start.2 = (f32[256]{0:T(256)S(1)}, f32[256]{0:T(256)}, u32[]{:S(2)}) copy-start(f32[256]{0:T(256)} %param.7) | copy-start | bytes 3076
Sparse Core Ops, SparseCore 0:
  10.7 79.9 all-gather.2
  101.2 79.4 reduce-scatter.1
  440.9 45.8 all-gather.4
where the time goes:
time: 809 us
  blocking collectives  578 us (71%)
  waiting for transfers between devices  170 us (21%)
  matrix products  29.2 us (4%)
  between operations  13.8 us (2%)
  local copies, waits for them, and re-layouts  9.86 us (1%)
    psum x1, blocking collectives, body(): summed = lax.psum(partial_input, 'vocab')  290 us
    pmax x1, blocking collectives, body(): lax.pmax((jnp.max(logits, axis=1), jnp.max(target_logits, axis=1)), 'vocab')  129 us
    psum x1, blocking collectives, body(): lax.psum((jnp.sum(student_exp, axis=1), jnp.sum(target_exp, axis=1)), 'vo...  124 us
    all_gather x1, waiting for transfers between devices, body(): rows_all = lax.all_gather(hidden, 'vocab', axis=0, tiled=True)  82.8 us
    all_gather x1, waiting for transfers between devices, body(): grad_all = lax.all_gather(grad_logits, 'tok', axis=0, tiled=True)  46 us
    reduce_scatter x1, waiting for transfers between devices, body(): lax.psum_scatter(jnp.dot(rows_all, head, preferred_element_type=jnp.float...  40.3 us
    all_to_all x1, blocking collectives, body(): lax.all_to_all(teacher, 'vocab', split_axis=1, concat_axis=0, tiled=True)  35.6 us
  transfers between devices with their start and end apart: 3, of which 3 were waited for; matrix products, arithmetic and copies ran while one was open for 0% of the time, Pallas kernels for 0%

commit v1 on v0

v1 whole, which is shorter than its diff:
```python
import jax
import jax.numpy as jnp
from jax import lax
from jax.experimental import pallas as pl
from jax.experimental.pallas import tpu as pltpu
from jax.sharding import PartitionSpec as P

MESH = pl.DeviceIdType.MESH
F32, BF16 = jnp.float32, jnp.bfloat16
NX, NZ, NY, NC = 4, 8, 4, 2
YC = NY * NC
RB = 16
POWER = 9


class Copies:
    def __init__(self, send, recv):
        self.send, self.recv, self.count, self.started = send, recv, 0, []

    def make(self, src, dst, vocab, tok):
        n = self.count
        self.count += 1
        return pltpu.make_async_remote_copy(
            src_ref=src,
            dst_ref=dst,
            send_sem=self.send.at[n],
            recv_sem=self.recv.at[n],
            device_id={"vocab": vocab, "tok": tok},
            device_id_type=MESH,
        )

    def start(self, src, dst, vocab, tok):
        copy = self.make(src, dst, vocab, tok)
        copy.start()
        self.started.append(copy)
        return copy


def encode(p):
    p2 = p * p
    p4 = p2 * p2
    return (p4 * p4 * p).astype(BF16)


def decode(x):
    x = x.astype(F32)
    root = jnp.exp(jnp.log(jnp.abs(x)) * (1.0 / POWER))
    return jnp.where(x < 0.0, -root, root)


def eye():
    return lax.broadcasted_iota(jnp.int32, (128, 128), 0) == lax.broadcasted_iota(jnp.int32, (128, 128), 1)


def to_row(wide):
    return jnp.sum(jnp.where(eye(), wide, 0.0), axis=0, keepdims=True)


def to_column(row):
    return jnp.sum(jnp.where(eye(), jnp.broadcast_to(row, (128, 128)), 0.0), axis=1, keepdims=True)


def tile(*rows):
    return jnp.concatenate(list(rows) + [jnp.zeros((8 - len(rows), 128), F32)], axis=0)


def merge(ref, h):
    peak = ref[h, 0, 0:1, :]
    tpeak = ref[h, 0, 2:3, :]
    for i in range(1, 8):
        peak = jnp.maximum(peak, ref[h, i, 0:1, :])
        tpeak = jnp.maximum(tpeak, ref[h, i, 2:3, :])
    total = jnp.zeros_like(peak)
    ttotal = jnp.zeros_like(peak)
    for i in range(8):
        total += ref[h, i, 1:2, :] * jnp.exp(ref[h, i, 0:1, :] - peak)
        ttotal += ref[h, i, 3:4, :] * jnp.exp(ref[h, i, 2:3, :] - tpeak)
    return peak, total, tpeak, ttotal


def kernel(
    hidden, head, teacher, weight, gh_out, gw_out,
    hid, headv, tmid, tfin, te, po, to_l, to_r, r_opp, from_l, from_r, own, acc_l, acc_r,
    stc, st0, st1, st1m, st2, fac, gbuf, acc, at, gwb,
    ghp, ghr, zs, zr, gho, local, send, recv, zsend, zrecv,
):
    v, me = lax.axis_index("vocab"), lax.axis_index("tok")
    z, yc = v // YC, v % YC
    y, c = yc // NC, yc % NC
    left, right, opp = (me + NX - 1) % NX, (me + 1) % NX, (me + 2) % NX
    blocks = (opp, right, left, me)
    width, cols = headv.shape
    chunk = min(512, cols)
    chunks = cols // chunk
    cp = Copies(send, recv)

    def zpeer(k):
        return ((z + k) % NZ) * YC + yc

    def ycpeer(k):
        return z * YC + (yc + k) % YC

    get_head = pltpu.make_async_copy(head, headv, local.at[0])
    get_head.start()
    get_hidden = pltpu.make_async_copy(hidden, hid.at[z, y, c], local.at[1])
    get_hidden.start()
    get_teacher = pltpu.make_async_copy(teacher.at[:, yc], tmid.at[yc], local.at[2])
    get_teacher.start()

    barrier = pltpu.get_barrier_semaphore()
    for k in range(1, NZ):
        pl.semaphore_signal(barrier, inc=1, device_id={"vocab": zpeer(k), "tok": me}, device_id_type=MESH)
    for k in range(1, YC):
        pl.semaphore_signal(barrier, inc=1, device_id={"vocab": ycpeer(k), "tok": me}, device_id_type=MESH)
    for x in (left, right):
        pl.semaphore_signal(barrier, inc=1, device_id={"vocab": v, "tok": x}, device_id_type=MESH)
    pl.semaphore_wait(barrier, NZ - 1 + YC - 1 + 2)

    hz = [cp.start(hidden, hid.at[z, y, c], zpeer(k), me) for k in range(1, NZ)]
    tyc = [cp.start(teacher.at[:, (yc + k) % YC], tmid.at[yc], ycpeer(k), me) for k in range(1, YC)]
    get_hidden.wait()
    for copy in hz:
        copy.wait_recv()
    hy = []
    for d in blocks:
        part = hid.at[pl.ds(2 * d, 2), y, c]
        hy.append([cp.start(part, part, ycpeer(NC * k), me) for k in range(1, NY)])

    def rows_of(j):
        for copy in hy[j]:
            copy.wait_recv()
        part = hid.at[pl.ds(2 * blocks[j], 2), :, c]
        return cp.start(part, part, ycpeer_sibling, me)

    ycpeer_sibling = z * YC + y * NC + (1 - c)

    def hidden_rows(d):
        return hid[pl.ds(2 * d, 2)].reshape(2 * YC * RB, width)

    def partial(j, write):
        def step(q, _):
            here = pl.ds(pl.multiple_of(q * chunk, chunk), chunk)
            p = jnp.dot(hidden_rows(blocks[j]), headv[:, here], preferred_element_type=F32)
            write(here, p)
            return 0

        lax.fori_loop(0, chunks, step, 0)

    def write_opp(here, p):
        po[:, :, :, here] = encode(p.reshape(2, 2, 64, chunk))

    def write_right(here, p):
        p = p.reshape(2, 2, 64, chunk)
        to_r[:, 0, :, here] = encode(p[:, 0])
        acc_r[:, :, here] = p[:, 1]

    def write_left(here, p):
        p = p.reshape(2, 2, 64, chunk)
        to_l[:, 1, :, here] = encode(p[:, 1])
        acc_l[:, :, here] = p[:, 0]

    def write_own(here, p):
        own[:, :, here] = p.reshape(2, 128, chunk)

    sib = rows_of(0)
    sib.wait_recv()
    get_head.wait()
    partial(0, write_opp)

    def send_opp(h):
        return (
            cp.start(po.at[h, 0], r_opp.at[h, 0], v, left),
            cp.start(po.at[h, 1], r_opp.at[h, 1], v, right),
        )

    opp0 = send_opp(0)
    get_teacher.wait()
    for copy in tyc:
        copy.wait_recv()
    keep_teacher = pltpu.make_async_copy(tmid.at[:, z], tfin.at[pl.ds(z * YC, YC)], local.at[3])
    keep_teacher.start()
    tz = [
        cp.start(tmid.at[:, (z + k) % NZ], tfin.at[pl.ds(z * YC, YC)], zpeer(k), me)
        for k in range(1, NZ)
    ]
    sib = rows_of(1)
    sib.wait_recv()
    partial(1, write_right)
    right0 = cp.start(to_r.at[0, 0], from_l.at[0, 0], v, right)
    sib = rows_of(2)
    sib.wait_recv()
    partial(2, write_left)
    left0 = cp.start(to_l.at[0, 1], from_r.at[0, 1], v, left)
    opp1 = send_opp(1)
    sib = rows_of(3)

    def add_opp(h):
        def step(g, _):
            here = pl.ds(pl.multiple_of(g * 16, 16), 16)
            to_l[h, 0, here] = encode(acc_l[h, here] + decode(r_opp[h, 0, here]))
            to_r[h, 1, here] = encode(acc_r[h, here] + decode(r_opp[h, 1, here]))
            return 0

        lax.fori_loop(0, 4, step, 0)

    def send_sum(h):
        return (
            cp.start(to_l.at[h, 0], from_r.at[h, 0], v, left),
            cp.start(to_r.at[h, 1], from_l.at[h, 1], v, right),
        )

    for copy in opp0:
        copy.wait_recv()
    add_opp(0)
    sum0 = send_sum(0)
    right1 = cp.start(to_r.at[1, 0], from_l.at[1, 0], v, right)
    left1 = cp.start(to_l.at[1, 1], from_r.at[1, 1], v, left)
    sib.wait_recv()
    partial(3, write_own)
    for copy in opp1:
        copy.wait_recv()
    add_opp(1)
    sum1 = send_sum(1)

    keep_teacher.wait()
    for copy in tz:
        copy.wait_recv()

    def teacher_pair(p, _):
        h, q = p // 16, p % 16
        low = lax.broadcasted_iota(jnp.int32, (8, 8, 128), 1) < 4
        a = tfin[2 * p].astype(F32).reshape(8, 8, 128)
        b = tfin[2 * p + 1].astype(F32).reshape(8, 8, 128)
        even = jnp.where(low, a, pltpu.roll(b, 4, 1))
        odd = jnp.where(low, pltpu.roll(a, 4, 1), b)
        peak = jnp.max(jnp.max(jnp.maximum(even, odd), axis=0), axis=1, keepdims=True)
        even, odd = jnp.exp(even - peak), jnp.exp(odd - peak)
        total = jnp.sum(jnp.sum(even + odd, axis=0), axis=1, keepdims=True)
        here = pl.ds(pl.multiple_of(q * 8, 8), 8)
        for k in range(8):
            te[h, here, 256 * k : 256 * k + 128] = even[k]
            te[h, here, 256 * k + 128 : 256 * k + 256] = odd[k]
        stc[h, 2, here] = jnp.broadcast_to(peak, (8, 128))
        stc[h, 3, here] = jnp.broadcast_to(total, (8, 128))
        return 0

    lax.fori_loop(0, 32, teacher_pair, 0)

    def gradient(h, arrivals):
        for copy in arrivals:
            copy.wait_recv()

        def student(g, _):
            here = pl.ds(pl.multiple_of(g * 16, 16), 16)
            inside = pl.ds(pl.multiple_of((g % 4) * 16, 16), 16)
            half = g // 4
            logits = own[h, here] + decode(from_l[h, half, inside]) + decode(from_r[h, half, inside])
            peak = jnp.max(logits, axis=1, keepdims=True)
            exps = jnp.exp(logits - peak)
            own[h, here] = exps
            stc[h, 0, here] = jnp.broadcast_to(peak, (16, 128))
            stc[h, 1, here] = jnp.broadcast_to(jnp.sum(exps, axis=1, keepdims=True), (16, 128))
            return 0

        lax.fori_loop(0, 8, student, 0)
        mine = tile(to_row(stc[h, 0]), to_row(stc[h, 1]), to_row(stc[h, 2]), to_row(stc[h, 3]))
        st0[h] = mine
        st1[h, z] = mine
        over_z = [cp.start(st0.at[h], st1.at[h, z], zpeer(k), me) for k in range(1, NZ)]
        for copy in over_z:
            copy.wait_recv()
        plane = tile(*merge(st1, h))
        st1m[h] = plane
        st2[h, yc] = plane
        over_yc = [cp.start(st1m.at[h], st2.at[h, yc], ycpeer(k), me) for k in range(1, YC)]
        for copy in over_yc:
            copy.wait_recv()
        peak, total, tpeak, ttotal = merge(st2, h)
        w = weight[h : h + 1, :]
        fac[0] = jnp.broadcast_to(to_column(w * jnp.exp(st0[h, 0:1, :] - peak) / total), (128, 128))
        fac[1] = jnp.broadcast_to(to_column(w * jnp.exp(st0[h, 2:3, :] - tpeak) / ttotal), (128, 128))

        def write(g, _):
            here = pl.ds(pl.multiple_of(g * 16, 16), 16)
            gbuf[me, h, here] = (fac[0, here, :1] * own[h, here] - fac[1, here, :1] * te[h, here]).astype(BF16)
            return 0

        lax.fori_loop(0, 8, write, 0)
        return (
            cp.start(gbuf.at[me, h], gbuf.at[me, h], v, left),
            cp.start(gbuf.at[me, h], gbuf.at[me, h], v, right),
        )

    all0 = gradient(0, (right0, left0) + sum0)
    all1 = gradient(1, (right1, left1) + sum1)

    def hidden_partial(j, d):
        g = gbuf[d].reshape(256, cols)
        for n in range(0, width, 256):
            m = min(256, width - n)
            part = lax.dot_general(
                g, headv[n : n + m, :], (((1,), (1,)), ((), ())), preferred_element_type=F32
            )
            ghp[j, :, :, :, n : n + m] = part.reshape(2, YC, RB, m).astype(BF16)
        return [cp.start(ghp.at[j, :, (yc + k) % YC], ghr.at[j, k], ycpeer(k), me) for k in range(1, YC)]

    def hidden_sum(j, d, copies):
        for copy in copies:
            copy.wait_recv()
        total = ghp[j, :, yc].astype(F32)
        for k in range(1, YC):
            total += ghr[j, k].astype(F32)
        zs[j] = total
        for h in range(2):
            goal = 2 * d + h
            k = (goal - z + NZ) % NZ

            @pl.when(k != 0)
            def _():
                z_copy(j, h, goal, k).start()

            @pl.when(k == 0)
            def _():
                zr[0] = zs[j, h]

    def z_copy(j, h, goal, k):
        return pltpu.make_async_remote_copy(
            src_ref=zs.at[j, h],
            dst_ref=zr.at[k],
            send_sem=zsend.at[2 * j + h],
            recv_sem=zrecv.at[k],
            device_id={"vocab": goal * YC + yc, "tok": me},
            device_id_type=MESH,
        )

    def head_update(d, first, last):
        at[...] = hidden_rows(d).T

        def step(q, _):
            here = pl.ds(pl.multiple_of(q * chunk, chunk), chunk)
            part = jnp.dot(at[...], gbuf[d, :, :, here].reshape(256, chunk), preferred_element_type=F32)
            if not first:
                part = part + acc[:, here]
            if last:
                gwb[:, here] = part.astype(BF16)
                pltpu.make_async_copy(gwb.at[:, here], gw_out.at[:, here], local.at[4 + q]).start()
            else:
                acc[:, here] = part
            return 0

        lax.fori_loop(0, chunks, step, 0)

    def forward(h):
        all1_or_0 = all0 if h == 0 else all1
        all1_or_0[0].wait_recv()
        a = cp.start(gbuf.at[right, h, pl.ds(0, 64)], gbuf.at[right, h, pl.ds(0, 64)], v, left)
        all1_or_0[1].wait_recv()
        b = cp.start(gbuf.at[left, h, pl.ds(64, 64)], gbuf.at[left, h, pl.ds(64, 64)], v, right)
        return a, b

    gh_me = hidden_partial(0, me)
    fwd0 = forward(0)
    head_update(me, True, False)
    fwd1 = forward(1)
    gh_right = hidden_partial(1, right)
    gh_left = hidden_partial(2, left)
    hidden_sum(0, me, gh_me)
    head_update(right, False, False)
    hidden_sum(1, right, gh_right)
    head_update(left, False, False)
    hidden_sum(2, left, gh_left)
    for copy in fwd0 + fwd1:
        copy.wait_recv()
    gh_opp = hidden_partial(3, opp)
    head_update(opp, False, True)
    hidden_sum(3, opp, gh_opp)
    for k in range(1, NZ):
        z_copy(0, 0, z, k).wait_recv()
    total = zr[0]
    for k in range(1, NZ):
        total = total + zr[k]
    gho[...] = total.astype(BF16)
    put = pltpu.make_async_copy(gho, gh_out, local.at[1])
    put.start()

    for copy in cp.started:
        copy.wait_send()
    for j, d in enumerate((me, right, left, opp)):
        for h in range(2):
            goal = 2 * d + h
            k = (goal - z + NZ) % NZ

            @pl.when(k != 0)
            def _():
                z_copy(j, h, goal, k).wait_send()

    for q in range(chunks):
        here = pl.ds(q * chunk, chunk)
        pltpu.make_async_copy(gwb.at[:, here], gw_out.at[:, here], local.at[4 + q]).wait()
    put.wait()


def body(hidden, head, teacher, token_weight):
    width, cols = head.shape
    lanes = cols // 128
    blocks = teacher.reshape(4, NZ * YC, lanes, 128).transpose(1, 2, 0, 3).reshape(NZ, YC, 4 * lanes, 128)
    hbm = pl.BlockSpec(memory_space=pl.ANY)
    half = pltpu.VMEM((2, 2, 64, cols), BF16)
    return pl.pallas_call(
        kernel,
        out_shape=(
            jax.ShapeDtypeStruct((RB, width), BF16),
            jax.ShapeDtypeStruct((width, cols), BF16),
        ),
        in_specs=[hbm, hbm, hbm, pl.BlockSpec(memory_space=pltpu.VMEM)],
        out_specs=(hbm, hbm),
        scratch_shapes=[
            pltpu.VMEM((NZ, NY, NC, RB, width), BF16),
            pltpu.VMEM((width, cols), BF16),
            pltpu.VMEM((YC, NZ, 4 * lanes, 128), BF16),
            pltpu.VMEM((NZ * YC, 4 * lanes, 128), BF16),
            pltpu.VMEM((2, 128, cols), F32),
            half, half, half, half, half, half,
            pltpu.VMEM((2, 128, cols), F32),
            pltpu.VMEM((2, 64, cols), F32),
            pltpu.VMEM((2, 64, cols), F32),
            pltpu.VMEM((2, 4, 128, 128), F32),
            pltpu.VMEM((2, 8, 128), F32),
            pltpu.VMEM((2, NZ, 8, 128), F32),
            pltpu.VMEM((2, 8, 128), F32),
            pltpu.VMEM((2, YC, 8, 128), F32),
            pltpu.VMEM((2, 128, 128), F32),
            pltpu.VMEM((NX, 2, 128, cols), BF16),
            pltpu.VMEM((width, cols), F32),
            pltpu.VMEM((width, 256), BF16),
            pltpu.VMEM((width, cols), BF16),
            pltpu.VMEM((4, 2, YC, RB, width), BF16),
            pltpu.VMEM((4, YC, 2, RB, width), BF16),
            pltpu.VMEM((4, 2, RB, width), F32),
            pltpu.VMEM((NZ, RB, width), F32),
            pltpu.VMEM((RB, width), BF16),
            pltpu.SemaphoreType.DMA((8,)),
            pltpu.SemaphoreType.DMA((128,)),
            pltpu.SemaphoreType.DMA((128,)),
            pltpu.SemaphoreType.DMA((8,)),
            pltpu.SemaphoreType.DMA((8,)),
        ],
        compiler_params=pltpu.CompilerParams(
            collective_id=0, has_side_effects=True, vmem_limit_bytes=56 * 1024 * 1024
        ),
        cost_estimate=pl.CostEstimate(flops=11_274_289_152, bytes_accessed=9_000_000, transcendentals=1_048_576),
    )(hidden, head, blocks, token_weight.reshape(2, 128))


def solution(mesh):
    return jax.shard_map(
        body,
        mesh=mesh,
        in_specs=(P("vocab", "tok"), P("tok", "vocab"), P(("tok", "vocab"), None), P("tok")),
        out_specs=(P("vocab", "tok"), P("tok", "vocab")),
        check_vma=False,
    )
```

time: 809 us -> 136 us (0.17)
  blocking collectives: 578 us -> 0 us
  waiting for transfers between devices: 170 us -> 0 us
  Pallas kernels: 0 us -> 127 us
  matrix products: 29.2 us -> 0 us
  between operations: 13.8 us -> 0.64 us
    psum x2 -> x0, blocking collectives: 414 us -> none  [the longest x1 290 us: body(): summed = lax.psum(partial_input, 'vocab')]
    pmax x1 -> x0, blocking collectives: 129 us -> none  [body(): lax.pmax((jnp.max(logits, axis=1), jnp.max(target_logits, axis=1)), 'vocab')]
    all_gather x2 -> x0, waiting for transfers between devices: 129 us -> none  [the longest x1 82.8 us: body(): rows_all = lax.all_gather(hidden, 'vocab', axis=0, tiled=True)]
    pallas_call x0 -> x1, Pallas kernels: none -> 127 us  [body(): pl.pallas_call(kernel, out_shape=(jax.ShapeDtypeStruct((RB, width), BF16)...]
    reduce_scatter x1 -> x0, waiting for transfers between devices: 40.3 us -> none  [body(): lax.psum_scatter(jnp.dot(rows_all, head, preferred_element_type=jnp.float...]
    all_to_all x1 -> x0, blocking collectives: 35.6 us -> none  [body(): lax.all_to_all(teacher, 'vocab', split_axis=1, concat_axis=0, tiled=True)]
    dot_general x3 -> x0, matrix products: 29.2 us -> none  [the longest x1 10.3 us: body(): jnp.dot(rows_all, head, preferred_element_type=jnp.float32)]
  transfers between devices with their start and end apart: 3 -> 0, of which waited for: 3 -> 0; matrix products, arithmetic and copies ran while one was open for 0% -> 0% of each run, Pallas kernels for 0% -> 0%
where the time goes in v1:
time: 136 us; the launch traced here: 134 us
  Pallas kernels  127 us (93%)
  local copies, waits for them, and re-layouts  5.73 us (4%)
    pallas_call x1, Pallas kernels, body(): pl.pallas_call(kernel, out_shape=(jax.ShapeDtypeStruct((RB, width), BF16)...  127 us
    unnamed x2, local copies, waits for them, and re-layouts  5.73 us

profile of v1, /device:TPU:2, one launch (start us, length us, event | category | flops | bytes accessed | tf_op | source)
XLA Modules:
  0.0 133.9 jit_solution(10313103639090455374)
XLA Ops:
  0.6 127.5 %shard_map.59 = (bf16[16,896]{1,0:T(8,128)(2,1)}, bf16[896,2048]{1,0:T(8,128)(2,1)}) custom-call(bf16[16,896]{1,0:T(8,128)(2,1)} %hidden.1, bf16[896,2048]{1,0:T(8,128)(2,1)} %head.1, bf16[8,8,64,128]{3,2,1,0:T(8,128)(2,1)} %bitcast.6, f32[2,128]{1,0:T(2,128)} %bitcast.7), custom_call_target="tpu_custom_call" | custom-call | flops 11274289152 | bytes 9000000 | tf_op jit(solution)/shard_map/pallas_call | solution.py:409
  128.1 1.4 %copy.9 = bf16[16,896]{1,0:T(8,128)(2,1)} copy(bf16[16,896]{1,0:T(8,128)(2,1)} %get-tuple-element.4) | data formatting | bytes 57344
  129.5 4.4 %copy.10 = bf16[896,2048]{1,0:T(8,128)(2,1)} copy(bf16[896,2048]{1,0:T(8,128)(2,1)} %get-tuple-element.5) | data formatting | bytes 7340032
